TPU v7x, 32 devices: a whole 2x2x4 slice. The times are simulated.
32 devices in a mesh: pair: 8 (over z, core), narrow: 4 (over y, x).
Axes of the slice: x: 2, y: 2, z: 4, core: 2. Of those that a mesh axis runs over, the one named last changes fastest.
Arguments:
- trial_slab: bfloat16 [8, 64, 10240], P(None, 'pair', 'narrow'), may hold values from -6 to 6
- ladder: bfloat16 [8192, 10240], P('pair', 'narrow'), may hold values from -0.0625 to 0.0625
- range_irreps: int32 [8], replicated, may hold values from 0 to 7, as said below
Outputs:
- sigma: bfloat16 [64, 8192], P(('pair', 'narrow'))
Inputs may be any that keep to these rules, and one draw needn't show every extreme that they name: `range_irreps`: non-decreasing along the pair index; the first entry is 0 and the last is 7.
All inputs are finite; a program needn't handle non-finite values.
Results may differ from a plain program's by a relative error of at most 0.019.
Values may be sent and summed in bfloat16 or wider, within the bound.
A program may use at most 64 MiB of HBM per device.

v0:
```python
import jax
import jax.numpy as jnp
from jax import lax
from jax.sharding import PartitionSpec as P


def body(trial_slab, ladder, range_irreps):
    pair_count = lax.axis_size("pair")
    narrow_count = lax.axis_size("narrow")
    rows_out = trial_slab.shape[1] // narrow_count
    local_pairs = ladder.shape[0]
    chosen = jnp.take(trial_slab, range_irreps, axis=0)
    arrived = lax.all_to_all(chosen, "pair", split_axis=0, concat_axis=0, tiled=True)
    products = jnp.einsum("pmc,ac->mpa", arrived, ladder, preferred_element_type=jnp.float32)
    summed = lax.psum_scatter(
        products.reshape(-1, local_pairs).astype(jnp.bfloat16),
        "narrow",
        scatter_dimension=0,
        tiled=True,
    )
    rounded = summed.reshape(rows_out, pair_count, local_pairs)
    owned = lax.all_to_all(rounded, "pair", split_axis=1, concat_axis=1, tiled=True)
    return owned.reshape(rows_out, pair_count * local_pairs)


def solution(mesh):
    placed = (P(None, "pair", "narrow"), P("pair", "narrow"), P())
    return jax.shard_map(
        body, mesh=mesh, in_specs=placed, out_specs=P(("pair", "narrow"), None), check_vma=False
    )
```

profile of v0, /device:TPU:0, one launch (start us, length us, event | category | flops | bytes accessed | tf_op | source)
XLA Modules:
  0.0 72.1 jit_solution(1219976127498226795)
XLA Ops:
  6.5 0.0 copy-start
  6.5 0.0 reduce-scatter.2.cloned.1.call-start
  6.5 0.7 compare_and_fusion
  7.2 0.7 compare_select_fusion
  7.9 0.0 copy-done
  7.9 0.6 gather_fusion
  8.5 0.1 broadcast_select_fusion
  8.6 17.3 %all_to_all.10 = bf16[8,8,2560]{2,1,0:T(8,128)(2,1)S(1)} all-to-all(bf16[8,8,2560]{2,1,0:T(8,128)(2,1)S(1)} %broadcast_select_fusion), channel_id=1, replica_groups=mesh['pair'=8,'narrow'=4] {'pair'}, dimensions={0} | all-to-all | bytes 655360 | tf_op jit(solution)/shard_map/all_to_all | solution.py:13
  25.9 4.2 %fusion.5 = bf16[8,8,1024]{2,0,1:T(8,128)(2,1)S(1)} fusion(bf16[8,8,2560]{2,1,0:T(8,128)(2,1)S(1)} %all_to_all.10, bf16[1024,2560]{1,0:T(8,128)(2,1)} %param.4), kind=kOutput, calls=%fused_computation.4 | convolution fusion | flops 335609856 | bytes 5701632 | tf_op jit(solution)/shard_map/pmc,ac->mpa/dot_general | solution.py:14
  30.0 0.7 copy.8
  30.8 0.0 reduce-scatter.2.cloned.1.call-update
  30.8 22.9 %reduce-scatter.2.cloned.1.call-done = bf16[16,1024]{1,0:T(8,128)(2,1)} async-done(((bf16[64,1024]{1,0:T(8,128)(2,1)}), bf16[16,1024]{1,0:T(8,128)(2,1)}) %reduce-scatter.2.cloned.1.call-update) | async-done | bytes 32784 | tf_op jit(solution)/shard_map/reduce_scatter | solution.py:15
  53.7 0.8 %copy.6 = bf16[2,8,1024]{2,0,1:T(2,128)(2,1)S(1)} copy(bf16[2,8,1024]{2,1,0:T(8,128)(2,1)} %bitcast.17) | data formatting | bytes 65536 | tf_op jit(solution)/shard_map/reshape | solution.py:21
  54.5 10.1 %all_to_all.11 = bf16[2,8,1024]{2,0,1:T(2,128)(2,1)S(1)} all-to-all(bf16[2,8,1024]{2,0,1:T(2,128)(2,1)S(1)} %copy.6), channel_id=1, replica_groups=mesh['pair'=8,'narrow'=4] {'pair'}, dimensions={1} | all-to-all | bytes 65536 | tf_op jit(solution)/shard_map/all_to_all | solution.py:22
  64.6 0.6 copy.10
  (1 shorter events, 0.0 us)
Async XLA Ops:
  6.5 1.4 %copy-start = (bf16[8,8,2560]{2,1,0:T(8,128)(2,1)S(1)}, bf16[8,8,2560]{2,1,0:T(8,128)(2,1)}, u32[]{:S(2)}) copy-start(bf16[8,8,2560]{2,1,0:T(8,128)(2,1)} %param.3) | copy-start | bytes 983044
  6.5 47.2 %reduce-scatter.2.cloned.1.call-start = ((), (), s32[]{:S(2)}) async-start(), calls=%async_computation.3 | async-start | bytes 163840 | tf_op jit(solution)/shard_map/reduce_scatter | solution.py:15
Sparse Core Ops, SparseCore 0:
  30.9 22.7 reduce-scatter.1
where the time goes:
time: 72.4 us; the launch traced here: 72.1 us
  blocking collectives  27.4 us (38%)
  waiting for transfers between devices  22.9 us (32%)
  between operations  13.4 us (19%)
  matrix products  4.17 us (6%)
  local copies, waits for them, and re-layouts  2.7 us (4%)
  other arithmetic  1.47 us (2%)
    reduce_scatter x1, waiting for transfers between devices, body(): lax.psum_scatter(products.reshape(-1, local_pairs).astype(jnp.bfloat16),...  22.9 us
    all_to_all x1, blocking collectives, body(): lax.all_to_all(chosen, 'pair', split_axis=0, concat_axis=0, tiled=True)  17.3 us
    all_to_all x1, blocking collectives, body(): lax.all_to_all(rounded, 'pair', split_axis=1, concat_axis=1, tiled=True)  10.1 us
    dot_general x1, matrix products, body(): jnp.einsum('pmc,ac->mpa', arrived, ladder, preferred_element_type=jnp.flo...  4.17 us
  transfers between devices with their start and end apart: 1, of which 1 were waited for; matrix products, arithmetic and copies ran while one was open for 0% of the time, Pallas kernels for 0%

commit v1 on v0

v1 whole, which is shorter than its diff:
```python
import functools

import jax
import jax.numpy as jnp
from jax import lax
from jax.experimental import pallas as pl
from jax.experimental.pallas import tpu as pltpu
from jax.sharding import PartitionSpec as P

MESH = pl.DeviceIdType.MESH
NT = (((1,), (1,)), ((), ()))


def kernel(
    pairs, narrows, chunks, group,
    irrep_ref, trial_hbm, ladder_hbm, out_ref,
    trial, chosen, arrived, ladder, acc, partial, parts, total, summed, owned,
    trial_sem, ladder_sem, send1, recv1, send2, recv2, send3, recv3,
):
    p, n = lax.axis_index("pair"), lax.axis_index("narrow")
    rows, width, own_rows = trial.shape[1], ladder.shape[2], trial.shape[1] // narrows
    local, lanes = ladder.shape[1], ladder.shape[1] // 128

    trial_copy = pltpu.make_async_copy(trial_hbm, trial, trial_sem)
    trial_copy.start()
    barrier = pltpu.get_barrier_semaphore()
    for d in range(1, pairs):
        pl.semaphore_signal(barrier, inc=1, device_id=(lax.rem(p + d, pairs), n), device_id_type=MESH)
    for d in range(1, narrows):
        pl.semaphore_signal(barrier, inc=1, device_id=(p, lax.rem(n + d, narrows)), device_id_type=MESH)
    ladder_copies = [
        pltpu.make_async_copy(ladder_hbm.at[:, pl.ds(c * width, width)], ladder.at[c], ladder_sem.at[c])
        for c in range(chunks)
    ]
    for copy in ladder_copies:
        copy.start()

    trial_copy.wait()
    for c in range(chunks):
        for q in range(pairs):
            chosen[c, q] = trial[irrep_ref[q], :, pl.ds(c * width, width)]
        arrived[c, p] = trial[irrep_ref[p], :, pl.ds(c * width, width)]
    pl.semaphore_wait(barrier, pairs + narrows - 2)

    def exchange(c, d):
        q = lax.rem(p + d, pairs)
        return pltpu.make_async_remote_copy(
            src_ref=chosen.at[c, q], dst_ref=arrived.at[c, p],
            send_sem=send1.at[c, d], recv_sem=recv1.at[c, d],
            device_id=(q, n), device_id_type=MESH,
        )

    for c in range(chunks):
        for d in range(1, pairs):
            exchange(c, d).start()

    for c in range(chunks):
        ladder_copies[c].wait()
        for d in range(1, pairs):
            exchange(c, d).wait_recv()

        def multiply(g):
            taken = arrived[c, pl.ds(g * group, group)].astype(jnp.float32)
            taken = taken.reshape(group * rows, width).astype(jnp.bfloat16)
            product = lax.dot_general(taken, ladder[c], NT, preferred_element_type=jnp.float32)
            at = pl.ds(g * group * rows, group * rows)
            for j in range(lanes):
                tile = product[:, j * 128:(j + 1) * 128]
                acc[j, at, :] = tile if c == 0 else acc[j, at, :] + tile

        if pairs == group:
            multiply(0)
        else:
            pl.loop(0, pairs // group)(multiply)

    for m in range(narrows):
        for j in range(lanes):
            piece = [acc[j, pl.ds(m * own_rows + k, pairs, stride=rows), :] for k in range(own_rows)]
            partial[m, j] = jnp.concatenate(piece, axis=0).astype(jnp.bfloat16)

    def reduce(d):
        m = lax.rem(n + d, narrows)
        return pltpu.make_async_remote_copy(
            src_ref=partial.at[m], dst_ref=parts.at[d],
            send_sem=send2.at[d], recv_sem=recv2.at[d],
            device_id=(p, m), device_id_type=MESH,
        )

    for d in range(1, narrows):
        reduce(d).start()
    value = partial[n].astype(jnp.float32)
    for d in range(1, narrows):
        reduce(d).wait_recv()
        value += parts[d].astype(jnp.float32)
    total[...] = value

    for q in range(pairs):
        for j in range(lanes):
            rounded = total[j, pl.ds(q, own_rows, stride=pairs), :].astype(jnp.bfloat16)
            summed[q, :, pl.ds(j * 128, 128)] = rounded

    def deliver(d):
        q = lax.rem(p + d, pairs)
        return pltpu.make_async_remote_copy(
            src_ref=summed.at[q], dst_ref=owned.at[p],
            send_sem=send3.at[d], recv_sem=recv3.at[d],
            device_id=(q, n), device_id_type=MESH,
        )

    for d in range(1, pairs):
        deliver(d).start()
    owned[p] = summed[p]
    for d in range(1, pairs):
        deliver(d).wait_recv()
    for q in range(pairs):
        out_ref[:, pl.ds(q * local, local)] = owned[q]

    for d in range(1, pairs):
        for c in range(chunks):
            exchange(c, d).wait_send()
        deliver(d).wait_send()
    for d in range(1, narrows):
        reduce(d).wait_send()


def body(trial_slab, ladder, range_irreps):
    pairs, narrows = lax.axis_size("pair"), lax.axis_size("narrow")
    irreps, rows, contracted = trial_slab.shape
    local = ladder.shape[0]
    chunks = 5 if contracted % (5 * 256) == 0 else 1
    width = contracted // chunks
    own_rows = rows // narrows
    group = min(pairs, max(1, 64 // rows))
    bf16, f32 = jnp.bfloat16, jnp.float32
    return pl.pallas_call(
        functools.partial(kernel, pairs, narrows, chunks, group),
        out_shape=jax.ShapeDtypeStruct((own_rows, pairs * local), bf16),
        in_specs=[
            pl.BlockSpec(memory_space=pltpu.SMEM),
            pl.BlockSpec(memory_space=pl.ANY),
            pl.BlockSpec(memory_space=pl.ANY),
        ],
        out_specs=pl.BlockSpec(memory_space=pltpu.VMEM),
        scratch_shapes=[
            pltpu.VMEM((irreps, rows, contracted), bf16),
            pltpu.VMEM((chunks, pairs, rows, width), bf16),
            pltpu.VMEM((chunks, pairs, rows, width), bf16),
            pltpu.VMEM((chunks, local, width), bf16),
            pltpu.VMEM((local // 128, pairs * rows, 128), f32),
            pltpu.VMEM((narrows, local // 128, own_rows * pairs, 128), bf16),
            pltpu.VMEM((narrows, local // 128, own_rows * pairs, 128), bf16),
            pltpu.VMEM((local // 128, own_rows * pairs, 128), f32),
            pltpu.VMEM((pairs, own_rows, local), bf16),
            pltpu.VMEM((pairs, own_rows, local), bf16),
            pltpu.SemaphoreType.DMA,
            pltpu.SemaphoreType.DMA((chunks,)),
            pltpu.SemaphoreType.DMA((chunks, pairs)),
            pltpu.SemaphoreType.DMA((chunks, pairs)),
            pltpu.SemaphoreType.DMA((narrows,)),
            pltpu.SemaphoreType.DMA((narrows,)),
            pltpu.SemaphoreType.DMA((pairs,)),
            pltpu.SemaphoreType.DMA((pairs,)),
        ],
        compiler_params=pltpu.CompilerParams(
            collective_id=0, has_side_effects=True, vmem_limit_bytes=48 * 1024 * 1024
        ),
    )(range_irreps, trial_slab, ladder)


def solution(mesh):
    placed = (P(None, "pair", "narrow"), P("pair", "narrow"), P())
    return jax.shard_map(
        body, mesh=mesh, in_specs=placed, out_specs=P(("pair", "narrow"), None), check_vma=False
    )
```

time: 72.4 us -> 29.2 us (0.40)
  blocking collectives: 27.4 us -> 0 us
  Pallas kernels: 0 us -> 24.2 us
  waiting for transfers between devices: 22.9 us -> 0 us
  between operations: 13.4 us -> 0.01 us
  matrix products: 4.17 us -> 0 us
  local copies, waits for them, and re-layouts: 2.7 us -> 4.73 us
  other arithmetic: 1.47 us -> 0 us
    all_to_all x2 -> x0, blocking collectives: 27.4 us -> none  [the longest x1 17.3 us: body(): lax.all_to_all(chosen, 'pair', split_axis=0, concat_axis=0, tiled=True)]
    pallas_call x0 -> x1, Pallas kernels: none -> 24.2 us  [body(): pl.pallas_call(functools.partial(kernel, pairs, narrows, chunks, group),...]
    reduce_scatter x1 -> x0, waiting for transfers between devices: 22.9 us -> none  [body(): lax.psum_scatter(products.reshape(-1, local_pairs).astype(jnp.bfloat16),...]
    dot_general x1 -> x0, matrix products: 4.17 us -> none  [body(): jnp.einsum('pmc,ac->mpa', arrived, ladder, preferred_element_type=jnp.flo...]
    unnamed x3 -> x7, local copies, waits for them, and re-layouts: 0.62 us -> 4.73 us
    reshape x1 -> x0, local copies, waits for them, and re-layouts: 0.79 us -> none  [body(): rounded = summed.reshape(rows_out, pair_count, local_pairs)]
    select_n x2 -> x0, other arithmetic: 0.76 us -> none  [body(): chosen = jnp.take(trial_slab, range_irreps, axis=0)]
  transfers between devices with their start and end apart: 1 -> 0, of which waited for: 1 -> 0; matrix products, arithmetic and copies ran while one was open for 0% -> 0% of each run, Pallas kernels for 0% -> 0%
where the time goes in v1:
time: 29.2 us; the launch traced here: 29 us
  Pallas kernels  24.2 us (83%)
  local copies, waits for them, and re-layouts  4.73 us (16%)
    pallas_call x1, Pallas kernels, body(): pl.pallas_call(functools.partial(kernel, pairs, narrows, chunks, group),...  24.2 us
    unnamed x7, local copies, waits for them, and re-layouts  4.73 us

profile of v1, /device:TPU:0, one launch (start us, length us, event | category | flops | bytes accessed | tf_op | source)
XLA Modules:
  0.0 29.0 jit_solution(9602372442255096130)
XLA Ops:
  0.0 0.0 copy-start
  0.0 2.5 %copy-done = bf16[1024,2560]{1,0:T(8,128)(2,1)S(1)} copy-done((bf16[1024,2560]{1,0:T(8,128)(2,1)S(1)}, bf16[1024,2560]{1,0:T(8,128)(2,1)}, u32[]{:S(2)}) %copy-start) | copy-done | bytes 5242904
  2.5 0.0 copy-start.1
  2.5 1.0 %copy-done.1 = bf16[8,8,2560]{2,1,0:T(8,128)(2,1)S(1)} copy-done((bf16[8,8,2560]{2,1,0:T(8,128)(2,1)S(1)}, bf16[8,8,2560]{2,1,0:T(8,128)(2,1)}, u32[]{:S(2)}) %copy-start.1) | copy-done | bytes 327704
  3.5 0.0 copy-start.2
  3.5 0.7 %copy-done.2 = s32[8]{0:T(128)S(1)} copy-done((s32[8]{0:T(128)S(1)}, s32[8]{0:T(128)}, u32[]{:S(2)}) %copy-start.2) | copy-done | bytes 56
  4.1 24.2 %shard_map.37 = bf16[2,8192]{1,0:T(2,128)(2,1)S(1)} custom-call(s32[8]{0:T(128)S(1)} %copy-done.2, bf16[8,8,2560]{2,1,0:T(8,128)(2,1)S(1)} %copy-done.1, bf16[1024,2560]{1,0:T(8,128)(2,1)S(1)} %copy-done), custom_call_target="tpu_custom_call" | custom-call | tf_op jit(solution)/shard_map/pallas_call | solution.py:135
  28.4 0.6 %copy.5 = bf16[2,8192]{1,0:T(2,128)(2,1)} copy(bf16[2,8192]{1,0:T(2,128)(2,1)S(1)} %shard_map.37) | data formatting | bytes 65536
Async XLA Ops:
  0.0 2.5 %copy-start = (bf16[1024,2560]{1,0:T(8,128)(2,1)S(1)}, bf16[1024,2560]{1,0:T(8,128)(2,1)}, u32[]{:S(2)}) copy-start(bf16[1024,2560]{1,0:T(8,128)(2,1)} %ladder_hbm.1) | copy-start | bytes 15728644
  2.5 1.0 %copy-start.1 = (bf16[8,8,2560]{2,1,0:T(8,128)(2,1)S(1)}, bf16[8,8,2560]{2,1,0:T(8,128)(2,1)}, u32[]{:S(2)}) copy-start(bf16[8,8,2560]{2,1,0:T(8,128)(2,1)} %trial_hbm.1) | copy-start | bytes 983044
  3.5 0.7 %copy-start.2 = (s32[8]{0:T(128)S(1)}, s32[8]{0:T(128)}, u32[]{:S(2)}) copy-start(s32[8]{0:T(128)} %irrep_ref.1) | copy-start | bytes 100

commit v2 on v1

v2 whole, which is shorter than its diff:
```python
import functools

import jax
import jax.numpy as jnp
from jax import lax
from jax.experimental import pallas as pl
from jax.experimental.pallas import tpu as pltpu
from jax.sharding import PartitionSpec as P

MESH = pl.DeviceIdType.MESH
NT = (((1,), (1,)), ((), ()))


def every(count, step):
    if count <= 8:
        for i in range(count):
            step(i)
    else:
        pl.loop(0, count)(step)


def kernel(
    pairs, narrows, chunks, group,
    irrep_hbm, trial_hbm, ladder_hbm, out_ref,
    irrep_ref, trial, chosen, arrived, ladder, acc, partial, parts, total,
    irrep_sem, trial_sem, ladder_sem, send1, recv1, send2, recv2,
):
    p, n = lax.axis_index("pair"), lax.axis_index("narrow")
    rows, width, own_rows = trial.shape[1], ladder.shape[2], trial.shape[1] // narrows
    local, lanes = ladder.shape[1], ladder.shape[1] // 128

    def each(step):
        every(narrows - 1, lambda e: step(0, e + 1))
        every(pairs - 1, lambda d: every(narrows, lambda e: step(d + 1, e)))

    def greet(d, e):
        peer = (lax.rem(p + d, pairs), lax.rem(n + e, narrows))
        pl.semaphore_signal(barrier, inc=1, device_id=peer, device_id_type=MESH)

    irrep_copy = pltpu.make_async_copy(irrep_hbm, irrep_ref, irrep_sem)
    irrep_copy.start()
    trial_copy = pltpu.make_async_copy(trial_hbm, trial, trial_sem)
    trial_copy.start()
    barrier = pltpu.get_barrier_semaphore()
    each(greet)
    ladder_copies = [
        pltpu.make_async_copy(ladder_hbm.at[:, pl.ds(c * width, width)], ladder.at[c], ladder_sem.at[c])
        for c in range(chunks)
    ]
    for copy in ladder_copies:
        copy.start()

    irrep_copy.wait()
    trial_copy.wait()
    for c in range(chunks):
        for q in range(pairs):
            chosen[c, q] = trial[irrep_ref[q], :, pl.ds(c * width, width)]
        arrived[c, p] = trial[irrep_ref[p], :, pl.ds(c * width, width)]
    pl.semaphore_wait(barrier, pairs * narrows - 1)

    def exchange(c, d):
        q = lax.rem(p + d, pairs)
        return pltpu.make_async_remote_copy(
            src_ref=chosen.at[c, q], dst_ref=arrived.at[c, p],
            send_sem=send1.at[c, d], recv_sem=recv1.at[c, d],
            device_id=(q, n), device_id_type=MESH,
        )

    for c in range(chunks):
        every(pairs - 1, lambda d: exchange(c, d + 1).start())

    for c in range(chunks):
        ladder_copies[c].wait()
        every(pairs - 1, lambda d: exchange(c, d + 1).wait_recv())

        def multiply(g):
            taken = arrived[c, pl.ds(g * group, group)].astype(jnp.float32)
            taken = taken.reshape(group * rows, width).astype(jnp.bfloat16)
            product = lax.dot_general(taken, ladder[c], NT, preferred_element_type=jnp.float32)
            for j in range(lanes):
                at = pl.ds(j * pairs * rows + g * group * rows, group * rows)
                tile = product[:, j * 128:(j + 1) * 128]
                acc[at, :] = tile if c == 0 else acc[at, :] + tile

        if pairs == group:
            multiply(0)
        else:
            pl.loop(0, pairs // group)(multiply)

    def pieces(q, m):
        first = q * rows + m * own_rows
        piece = [acc[pl.ds(first + k, lanes, stride=pairs * rows), :] for k in range(own_rows)]
        partial[q, m] = jnp.concatenate(piece, axis=0).astype(jnp.bfloat16)

    def deliver(d, e):
        q, m = lax.rem(p + d, pairs), lax.rem(n + e, narrows)
        return pltpu.make_async_remote_copy(
            src_ref=partial.at[q, m], dst_ref=parts.at[p, n],
            send_sem=send2.at[d, e], recv_sem=recv2.at[d, e],
            device_id=(q, m), device_id_type=MESH,
        )

    every(pairs, lambda q: every(narrows, lambda m: pieces(q, m)))
    each(lambda d, e: deliver(d, e).start())
    parts[p, n] = partial[p, n]
    each(lambda d, e: deliver(d, e).wait_recv())

    def add(q):
        value = parts[q, 0].astype(jnp.float32)
        for m in range(1, narrows):
            value += parts[q, m].astype(jnp.float32)
        total[q] = value
        for j in range(lanes):
            at = pl.ds(pl.multiple_of(q * local + j * 128, 128), 128)
            out_ref[:, at] = total[q, pl.ds(j, own_rows, stride=lanes), :].astype(jnp.bfloat16)

    every(pairs, add)

    for c in range(chunks):
        every(pairs - 1, lambda d: exchange(c, d + 1).wait_send())
    each(lambda d, e: deliver(d, e).wait_send())


def body(trial_slab, ladder, range_irreps):
    pairs, narrows = lax.axis_size("pair"), lax.axis_size("narrow")
    irreps, rows, contracted = trial_slab.shape
    local = ladder.shape[0]
    chunks = 5 if contracted % (5 * 256) == 0 else 1
    width = contracted // chunks
    own_rows = rows // narrows
    group = min(pairs, max(1, 64 // rows))
    bf16, f32 = jnp.bfloat16, jnp.float32
    return pl.pallas_call(
        functools.partial(kernel, pairs, narrows, chunks, group),
        out_shape=jax.ShapeDtypeStruct((own_rows, pairs * local), bf16),
        in_specs=[pl.BlockSpec(memory_space=pltpu.HBM)] * 3,
        out_specs=pl.BlockSpec(memory_space=pltpu.VMEM),
        scratch_shapes=[
            pltpu.SMEM(range_irreps.shape, jnp.int32),
            pltpu.VMEM((irreps, rows, contracted), bf16),
            pltpu.VMEM((chunks, pairs, rows, width), bf16),
            pltpu.VMEM((chunks, pairs, rows, width), bf16),
            pltpu.VMEM((chunks, local, width), bf16),
            pltpu.VMEM((local // 128 * pairs * rows, 128), f32),
            pltpu.VMEM((pairs, narrows, own_rows * local // 128, 128), bf16),
            pltpu.VMEM((pairs, narrows, own_rows * local // 128, 128), bf16),
            pltpu.VMEM((pairs, own_rows * local // 128, 128), f32),
            pltpu.SemaphoreType.DMA,
            pltpu.SemaphoreType.DMA,
            pltpu.SemaphoreType.DMA((chunks,)),
            pltpu.SemaphoreType.DMA((chunks, pairs)),
            pltpu.SemaphoreType.DMA((chunks, pairs)),
            pltpu.SemaphoreType.DMA((pairs, narrows)),
            pltpu.SemaphoreType.DMA((pairs, narrows)),
        ],
        compiler_params=pltpu.CompilerParams(
            collective_id=0, has_side_effects=True, vmem_limit_bytes=60 * 1024 * 1024
        ),
    )(range_irreps, trial_slab, ladder)


def solution(mesh):
    placed = (P(None, "pair", "narrow"), P("pair", "narrow"), P())
    return jax.shard_map(
        body, mesh=mesh, in_specs=placed, out_specs=P(("pair", "narrow"), None), check_vma=False
    )
```

time: 29.2 us -> 24.1 us (0.83)
  local copies, waits for them, and re-layouts: 4.73 us -> 1.4 us
  Pallas kernels: 24.2 us -> 22.5 us
    unnamed x7 -> x1, local copies, waits for them, and re-layouts: 4.73 us -> 1.4 us
    pallas_call x1, Pallas kernels: 24.2 us -> 22.5 us  [body(): pl.pallas_call(functools.partial(kernel, pairs, narrows, chunks, group),...]
where the time goes in v2:
time: 24.1 us; the launch traced here: 23.9 us
  Pallas kernels  22.5 us (93%)
  local copies, waits for them, and re-layouts  1.4 us (6%)
    pallas_call x1, Pallas kernels, body(): pl.pallas_call(functools.partial(kernel, pairs, narrows, chunks, group),...  22.5 us
    unnamed x1, local copies, waits for them, and re-layouts  1.4 us

profile of v2, /device:TPU:0, one launch (start us, length us, event | category | flops | bytes accessed | tf_op | source)
XLA Modules:
  0.0 23.9 jit_solution(18039274000238231931)
XLA Ops:
  0.0 22.5 %shard_map.37 = bf16[2,8192]{1,0:T(2,128)(2,1)} custom-call(s32[8]{0:T(128)} %irrep_hbm.1, bf16[8,8,2560]{2,1,0:T(8,128)(2,1)} %trial_hbm.1, bf16[1024,2560]{1,0:T(8,128)(2,1)} %ladder_hbm.1), custom_call_target="tpu_custom_call" | custom-call | tf_op jit(solution)/shard_map/pallas_call | solution.py:133
  22.5 1.4 %copy.5 = bf16[2,8192]{1,0:T(2,128)(2,1)} copy(bf16[2,8192]{1,0:T(2,128)(2,1)} %shard_map.37) | data formatting | bytes 65536
